TPU v7x, 256 devices: a whole 4x4x8 slice. The times are simulated.
256 devices in a mesh: dp: 32 (over x, z_hi, core), expert: 8 (over z_lo, y).
Axes of the slice: x: 4, y: 4, z: 8 (z_hi: 4, z_lo: 2; z = z_hi * 2 + z_lo), core: 2. Of those that a mesh axis runs over, the one named last changes fastest.
Arguments:
- grad_output: bfloat16 [32768, 6144], P(('dp', 'expert')), may hold values from -0.59765625 to 0.59765625
- hidden: bfloat16 [32, 8, 8, 48, 1024], P('dp', 'expert'), may hold values from -6 to 6
- probs: bfloat16 [32768, 2], P(('dp', 'expert')), may hold values from 0.099609375 to 0.8984375
- expert_ids: int32 [32768, 2], P(('dp', 'expert')), may hold values from 0 to 7, all different within a row; in each aligned block of 128 rows (0 to 127, 128 to 255, ...) at most 48 rows name the same one
- master: float32 [8, 1024, 6144], P('expert', 'dp'), may hold values from -0.1875 to 0.1875
- first_moment: float32 [8, 1024, 6144], P('expert', 'dp'), may hold values from -12 to 12
- second_moment: float32 [8, 1024, 6144], P('expert', 'dp'), may hold values from 1 to 40
Outputs:
- grad_hidden: bfloat16 [32, 8, 8, 48, 1024], P('dp', 'expert')
- grad_probs: float32 [32768, 2], P(('dp', 'expert'))
- new_master: float32 [8, 1024, 6144], P('expert', 'dp')
- new_first: float32 [8, 1024, 6144], P('expert', 'dp')
- new_second: float32 [8, 1024, 6144], P('expert', 'dp')
Inputs may be any that keep to these rules, and one draw needn't show every extreme that they name: `expert_ids`: in the rows of one device (aligned blocks of 128 tokens) each expert is named by at most 48 tokens, a bound that some block reaches; a token's two experts differ.
All inputs are finite; a program needn't handle non-finite values.
Results may differ from a plain program's by a relative error of at most 0.007.
Values may be sent and summed in bfloat16 or wider, within the bound.
A program may use at most 128 MiB of HBM per device.

v0:
```python
import jax
import jax.numpy as jnp
from jax import lax
from jax.sharding import PartitionSpec as P


def per_device(grad_output, hidden, probs, expert_ids, master, first_moment, second_moment):
    tok_rows = grad_output.shape[0]
    experts_here = lax.axis_size("expert")
    capacity = hidden.shape[3]
    slab_width = hidden.shape[4]
    model_width = grad_output.shape[1]
    routed_rows = experts_here * capacity
    flat_ids = expert_ids.reshape(-1)
    flat_probs = probs.reshape(-1)
    onehot = (flat_ids[:, None] == jnp.arange(experts_here, dtype=jnp.int32)[None, :]).astype(
        jnp.int32
    )
    slots = jnp.sum((jnp.cumsum(onehot, axis=0) - onehot) * onehot, axis=1)
    target = flat_ids * capacity + slots
    matches = target[None, :] == jnp.arange(routed_rows, dtype=jnp.int32)[:, None]
    filled = jnp.any(matches, axis=1)
    pair_token = jnp.arange(2 * tok_rows, dtype=jnp.int32) // 2
    source_row = jnp.sum(jnp.where(matches, pair_token[None, :], 0), axis=1)
    send_rows = jnp.where(filled[:, None], grad_output[source_row], jnp.zeros((), jnp.bfloat16))
    send_probs = jnp.sum(
        jnp.where(matches, flat_probs[None, :].astype(jnp.float32), 0.0), axis=1
    ).astype(jnp.bfloat16)
    got_rows, got_probs = (
        lax.all_to_all(
            send_rows.reshape(experts_here, capacity, model_width),
            "expert",
            split_axis=0,
            concat_axis=0,
            tiled=True,
        ),
        lax.all_to_all(
            send_probs.reshape(experts_here, capacity),
            "expert",
            split_axis=0,
            concat_axis=0,
            tiled=True,
        ),
    )
    routed = got_rows.reshape(routed_rows, model_width)
    scaled = (
        got_probs.reshape(routed_rows, 1).astype(jnp.float32) * routed.astype(jnp.float32)
    ).astype(jnp.bfloat16)
    activations = hidden.reshape(routed_rows, slab_width)
    weights_b = master[0].astype(jnp.bfloat16)
    gathered = lax.all_gather(weights_b, "dp", axis=0, tiled=True)
    expert_out = jnp.dot(activations, gathered, preferred_element_type=jnp.float32)
    grad_hid = lax.dot_general(
        scaled, gathered, (((1,), (1,)), ((), ())), preferred_element_type=jnp.float32
    )
    expert_out, grad_hid = (expert_out, grad_hid)
    grad = lax.psum_scatter(
        lax.dot_general(
            activations, scaled, (((0,), (0,)), ((), ())), preferred_element_type=jnp.float32
        ).astype(jnp.bfloat16),
        "dp",
        scatter_dimension=0,
        tiled=True,
    ).astype(jnp.float32)
    row_grad = jnp.sum(routed.astype(jnp.float32) * expert_out, axis=1).reshape(
        experts_here, capacity
    )
    back = lax.all_to_all(row_grad, "expert", split_axis=0, concat_axis=0, tiled=True)
    grad_probs = back.reshape(-1)[target].reshape(tok_rows, 2)
    grad_hidden = grad_hid.astype(jnp.bfloat16).reshape(hidden.shape)
    grad = grad.reshape(master.shape)
    new_first = 0.9 * first_moment + 0.1 * grad
    new_second = 0.95 * second_moment + 0.05 * grad * grad
    first_hat = new_first / (1.0 - 0.9**50)
    second_hat = new_second / (1.0 - 0.95**50)
    new_master = master - 0.0003 * (first_hat / (jnp.sqrt(second_hat) + 1e-08) + 0.1 * master)
    return (grad_hidden, grad_probs, new_master, new_first, new_second)


def solution(mesh):
    in_specs = (
        P(("dp", "expert"), None),
        P("dp", "expert", None, None, None),
        P(("dp", "expert"), None),
        P(("dp", "expert"), None),
        P("expert", "dp", None),
        P("expert", "dp", None),
        P("expert", "dp", None),
    )
    out_specs = (
        P("dp", "expert", None, None, None),
        P(("dp", "expert"), None),
        P("expert", "dp", None),
        P("expert", "dp", None),
        P("expert", "dp", None),
    )
    return jax.shard_map(
        per_device, mesh=mesh, in_specs=in_specs, out_specs=out_specs, check_vma=False
    )
```

profile of v0, /device:TPU:1, one launch (start us, length us, event | category | flops | bytes accessed | tf_op | source)
XLA Modules:
  0.0 398.0 jit_solution(5170909205910633490)
XLA Ops:
  7.2 0.0 copy-start
  7.2 0.9 copy.69
  8.1 0.1 eq.39
  8.2 0.1 reshape.169
  8.4 0.6 reduce-window.6
  9.0 0.2 slice_reduce_fusion
  9.2 0.1 fusion.18
  9.3 0.8 copy.71
  10.1 0.1 reshape.175
  10.2 0.2 select_reduce_fusion.1
  10.4 0.7 convert_element_type.111
  11.1 6.4 %all-to-all-start = ((bf16[8,1,48]{2,1,0:T(2,128)(2,1)}), bf16[8,1,48]{2,1,0:T(2,128)(2,1)S(1)}, u32[]{:S(2)}, u32[]{:S(2)}) async-start(bf16[8,1,48]{2,1,0:T(2,128)(2,1)} %convert_element_type.111), calls=%async_computation | async-start | bytes 8192 | tf_op jit(solution)/shard_map/all_to_all | solution.py:37
  17.5 0.1 fusion.16
  17.6 0.1 select_reduce_fusion
  17.8 0.1 broadcast_in_dim.47
  17.9 0.0 copy-done
  17.9 5.6 %gather_fusion = bf16[384,6144]{1,0:T(8,128)(2,1)} fusion(bf16[128,6144]{1,0:T(8,128)(2,1)S(1)} %copy-done, s32[1024]{0:T(1024)S(1)} %pad_clamp_fusion.1), kind=kCustom, calls=%fused_computation | custom fusion | bytes 9438720 | tf_op jit(solution)/shard_map/gather | solution.py:25
  23.5 4.8 %broadcast_select_fusion = bf16[8,48,6144]{2,1,0:T(8,128)(2,1)} fusion(bf16[8,48,6144]{2,1,0:T(8,128)(2,1)} %bitcast.48, pred[8,48]{1,0:T(8,128)(4,1)S(1)} %broadcast_in_dim.47), kind=kLoop, calls=%fused_computation.13 | loop fusion | flops 2359296 | bytes 9437568 | tf_op jit(solution)/shard_map/jit(_where)/select_n | solution.py:25
  28.4 0.0 all-to-all-done
  28.4 5.1 %all-to-all-start.1 = ((bf16[8,48,6144]{2,1,0:T(8,128)(2,1)}), bf16[8,48,6144]{2,1,0:T(8,128)(2,1)}, u32[]{:S(2)}, u32[]{:S(2)}) async-start(bf16[8,48,6144]{2,1,0:T(8,128)(2,1)} %broadcast_select_fusion), calls=%async_computation.1 | async-start | bytes 9437184 | tf_op jit(solution)/shard_map/all_to_all | solution.py:30
  33.5 0.0 reduce-scatter.4.cloned.1.call-start
  33.6 54.3 %all-to-all-done.1 = bf16[8,48,6144]{2,1,0:T(8,128)(2,1)} async-done(((bf16[8,48,6144]{2,1,0:T(8,128)(2,1)}), bf16[8,48,6144]{2,1,0:T(8,128)(2,1)}, u32[]{:S(2)}, u32[]{:S(2)}) %all-to-all-start.1) | async-done | bytes 4718624 | tf_op jit(solution)/shard_map/all_to_all | solution.py:30
  87.8 3.9 fusion.4
  91.7 9.6 %convert_bitcast_fusion = bf16[1024,6144]{0,1:T(8,128)(2,1)} fusion(bf16[384,6144]{1,0:T(8,128)(2,1)S(1)} %bitcast.49, bf16[384,1024]{1,0:T(8,128)(2,1)S(1)} %bitcast.53), kind=kOutput, calls=%fused_computation.6 | convolution fusion | flops 4838129664 | bytes 18087936 | tf_op jit(solution)/shard_map/dot_general | solution.py:58
  101.4 16.7 %copy.76 = bf16[1024,6144]{1,0:T(8,128)(2,1)} copy(bf16[1024,6144]{0,1:T(8,128)(2,1)} %convert_bitcast_fusion) | data formatting | bytes 25165824
  118.1 0.0 reduce-scatter.4.cloned.1.call-update
  118.1 0.0 copy-start.5
  118.1 0.2 all-gather.3.cloned.1.call-start
  118.4 142.1 %reduce-scatter.4.cloned.1.call-done = bf16[32,6144]{1,0:T(8,128)(2,1)} async-done(((bf16[1024,6144]{1,0:T(8,128)(2,1)}), bf16[32,6144]{1,0:T(8,128)(2,1)}) %reduce-scatter.4.cloned.1.call-update) | async-done | bytes 393232 | tf_op jit(solution)/shard_map/reduce_scatter | solution.py:57
  260.5 0.0 copy-done.4
  260.5 2.9 multiply_subtract_fusion
  263.4 0.0 all-gather.3.cloned.1.call-update
  263.4 0.1 copy.73
  263.6 0.1 mul.91
  263.7 0.1 reshape.176
  263.8 6.0 %fusion.5 = bf16[384,6144]{1,0:T(8,128)(2,1)} fusion(bf16[8,48,6144]{2,1,0:T(8,128)(2,1)} %all-to-all-done.1, f32[384]{0:T(512)S(1)} %reshape.176), kind=kLoop, calls=%fused_computation.11 | loop fusion | flops 7077888 | bytes 9438720 | tf_op jit(solution)/shard_map/convert_element_type | solution.py:48
  269.8 86.9 %all-gather.3.cloned.1.call-done = bf16[1,1024,6144]{2,1,0:T(8,128)(2,1)} async-done(((bf16[1,32,6144]{2,1,0:T(8,128)(2,1)}), bf16[1,1024,6144]{2,1,0:T(8,128)(2,1)}) %all-gather.3.cloned.1.call-update) | async-done | bytes 12582928 | tf_op jit(solution)/shard_map/all_gather | solution.py:51
  356.7 8.9 %fusion.6 = f32[384]{0:T(512)S(1)} fusion(bf16[8,48,6144]{2,1,0:T(8,128)(2,1)} %all-to-all-done.1, bf16[384,1024]{1,0:T(8,128)(2,1)S(1)} %bitcast.54, bf16[1,1024,6144]{2,1,0:T(8,128)(2,1)} %all-gather.3.cloned.1.call-done), kind=kOutput, calls=%fused_computation.12 | convolution fusion | flops 4838915584 | bytes 18089472 | tf_op jit(solution)/shard_map/dot_general | solution.py:52
  365.6 0.7 all_to_all.15
  366.3 10.6 %all-to-all-start.2 = ((f32[8,1,48]{2,1,0:T(1,128)}), f32[8,1,48]{2,1,0:T(1,128)S(1)}, u32[]{:S(2)}, u32[]{:S(2)}) async-start(f32[8,1,48]{2,1,0:T(1,128)} %all_to_all.15), calls=%async_computation.2 | async-start | bytes 8192 | tf_op jit(solution)/shard_map/all_to_all | solution.py:68
  376.9 10.3 %fusion.9 = bf16[384,1024]{1,0:T(8,128)(2,1)} fusion(bf16[384,6144]{1,0:T(8,128)(2,1)} %fusion.5, bf16[1,1024,6144]{2,1,0:T(8,128)(2,1)} %all-gather.3.cloned.1.call-done), kind=kOutput, calls=%fused_computation.14 | convolution fusion | flops 4832231424 | bytes 18087936 | tf_op jit(solution)/shard_map/dot_general | solution.py:53
  387.2 0.0 all-to-all-done.2
  387.2 0.5 broadcast.122
  387.7 0.7 reduce.11
  388.4 0.1 reshape.173
  388.4 1.9 gather_fusion.1
  390.4 0.1 reshape.174
  390.5 0.6 copy.75
  (21 shorter events, 0.1 us)
Async XLA Ops:
  7.2 10.7 %copy-start = (bf16[128,6144]{1,0:T(8,128)(2,1)S(1)}, bf16[128,6144]{1,0:T(8,128)(2,1)}, u32[]{:S(2)}) copy-start(bf16[128,6144]{1,0:T(8,128)(2,1)} %param.7) | copy-start | bytes 4718596
  11.1 17.3 %all-to-all-start = ((bf16[8,1,48]{2,1,0:T(2,128)(2,1)}), bf16[8,1,48]{2,1,0:T(2,128)(2,1)S(1)}, u32[]{:S(2)}, u32[]{:S(2)}) async-start(bf16[8,1,48]{2,1,0:T(2,128)(2,1)} %convert_element_type.111), calls=%async_computation | async-start | bytes 8192 | tf_op jit(solution)/shard_map/all_to_all | solution.py:37
  28.4 59.5 %all-to-all-start.1 = ((bf16[8,48,6144]{2,1,0:T(8,128)(2,1)}), bf16[8,48,6144]{2,1,0:T(8,128)(2,1)}, u32[]{:S(2)}, u32[]{:S(2)}) async-start(bf16[8,48,6144]{2,1,0:T(8,128)(2,1)} %broadcast_select_fusion), calls=%async_computation.1 | async-start | bytes 9437184 | tf_op jit(solution)/shard_map/all_to_all | solution.py:30
  33.5 227.0 %reduce-scatter.4.cloned.1.call-start = ((), (), s32[]{:S(2)}) async-start(), calls=%async_computation.5 | async-start | bytes 12976128 | tf_op jit(solution)/shard_map/reduce_scatter | solution.py:57
  87.8 3.9 copy-start.6
  118.1 142.4 %copy-start.2 = (f32[1,32,6144]{2,1,0:T(8,128)S(1)}, f32[1,32,6144]{2,1,0:T(8,128)}, u32[]{:S(2)}) copy-start(f32[1,32,6144]{2,1,0:T(8,128)} %param.11) | copy-start | bytes 2359300
  118.1 142.4 %copy-start.3 = (f32[1,32,6144]{2,1,0:T(8,128)S(1)}, f32[1,32,6144]{2,1,0:T(8,128)}, u32[]{:S(2)}) copy-start(f32[1,32,6144]{2,1,0:T(8,128)} %param.12) | copy-start | bytes 2359300
  118.1 142.4 %copy-start.4 = (f32[1,32,6144]{2,1,0:T(8,128)S(1)}, f32[1,32,6144]{2,1,0:T(8,128)}, u32[]{:S(2)}) copy-start(f32[1,32,6144]{2,1,0:T(8,128)} %param.13) | copy-start | bytes 2359300
  118.1 145.3 %copy-start.5 = (s32[128,2]{0,1:T(2,128)S(1)}, s32[128,2]{0,1:T(2,128)}, u32[]{:S(2)}) copy-start(s32[128,2]{0,1:T(2,128)} %param.10) | copy-start | bytes 3076
  118.1 238.6 %all-gather.3.cloned.1.call-start = ((), (), s32[]{:S(2)}) async-start(), calls=%async_computation.4 | async-start | bytes 12976128 | tf_op jit(solution)/shard_map/all_gather | solution.py:51
  366.3 20.9 %all-to-all-start.2 = ((f32[8,1,48]{2,1,0:T(1,128)}), f32[8,1,48]{2,1,0:T(1,128)S(1)}, u32[]{:S(2)}, u32[]{:S(2)}) async-start(f32[8,1,48]{2,1,0:T(1,128)} %all_to_all.15), calls=%async_computation.2 | async-start | bytes 8192 | tf_op jit(solution)/shard_map/all_to_all | solution.py:68
  376.9 14.3 %copy-start.1 = (bf16[128,6144]{1,0:T(8,128)(2,1)S(1)}, bf16[128,6144]{1,0:T(8,128)(2,1)}, u32[]{:S(2)}) copy-start(bf16[128,6144]{1,0:T(8,128)(2,1)} %param.7) | copy-start | bytes 4718596
Sparse Core Ops, SparseCore 0:
  118.2 142.1 reduce-scatter.3
  263.9 92.7 all-gather.2
where the time goes:
time: 399 us; the launch traced here: 398 us
  waiting for transfers between devices  283 us (71%)
  local copies, waits for them, and re-layouts  29.8 us (7%)
  matrix products  28.8 us (7%)
  starting transfers between devices  22.4 us (6%)
  other arithmetic  19.5 us (5%)
  between operations  14.2 us (4%)
    reduce_scatter x1, waiting for transfers between devices, per_device(): lax.psum_scatter(lax.dot_general(activations, scaled, (((0,), (0,)), ((),...  142 us
    all_gather x1, waiting for transfers between devices, per_device(): gathered = lax.all_gather(weights_b, 'dp', axis=0, tiled=True)  86.9 us
    all_to_all x1, waiting for transfers between devices, per_device(): lax.all_to_all(send_rows.reshape(experts_here, capacity, model_width), 'e...  54.3 us
    unnamed x17, local copies, waits for them, and re-layouts  18.3 us
    all_to_all x1, starting transfers between devices, per_device(): lax.all_to_all(row_grad, 'expert', split_axis=0, concat_axis=0, tiled=True)  10.6 us
    dot_general x1, matrix products, per_device(): lax.dot_general(scaled, gathered, (((1,), (1,)), ((), ())), preferred_ele...  10.3 us
    convert_element_type x2, other arithmetic, per_device(): scaled = (got_probs.reshape(routed_rows, 1).astype(jnp.float32) * routed....  9.85 us
    dot_general x1, matrix products, per_device(): lax.dot_general(activations, scaled, (((0,), (0,)), ((), ())), preferred_...  9.63 us
  transfers between devices with their start and end apart: 5, of which 3 were waited for; matrix products, arithmetic and copies ran while one was open for 7% of the time, Pallas kernels for 0%

commit v1 on v0

v1 whole, which is shorter than its diff:
```python
import jax
import jax.numpy as jnp
from jax import lax
from jax.experimental import pallas as pl
from jax.experimental.pallas import tpu as pltpu
from jax.sharding import PartitionSpec as P

MESH = pl.DeviceIdType.MESH
F32 = jnp.float32
BF16 = jnp.bfloat16
CAP = 48
WIDTHS = [128, 128, 256, 256, 256, 256, 128, 128]


def kernel(
    ids_ref, prob_ref, g_ref, hid_hbm, mas_hbm,
    gh_ref, gp_ref, gr_ref,
    INF, INE, T, SO, SB, RB, PC, HID, MAS, HQ, HT, WB, WQ, PX, PO, XR, ZS, ZR, FS, FR,
    GS1, GR1, GO1, GX, GR2, GO, RG, BK,
    l_s, is_s, is_r, ie_s, ie_r, iz_s, iz_r, q_s, q_r, z_s, z_r, y_s, y_r, y_l, x_s, x_r, zh_s, zh_r,
    f_s, f_r, h_s, h_r, w_s, w_r, wz_s, wz_r, wf_s, wf_r, wx_s, wx_r, g1_s, g1_r, g2_s, g2_r, b_s, b_r,
):
    QW = RB.shape[4]
    NC = len(WIDTHS)
    OFF = [sum(WIDTHS[:k]) for k in range(NC)]
    dp = lax.axis_index("dp")
    ex = lax.axis_index("expert")
    x, zh, c = dp // 8, (dp // 2) % 4, dp % 2
    zl, y = ex // 4, ex % 4
    px, xl = x // 2, x % 2
    h = (xl + px) % 2
    s = h * 2 + c
    xp = px * 2 + (1 - xl)

    def dev(x_, zh_, c_, zl_, y_):
        return ((x_ * 4 + zh_) * 2 + c_, zl_ * 4 + y_)

    mate_dev = [dev(x, zh, 1 - c, zl, y), dev(xp, zh, c, zl, y), dev(xp, zh, 1 - c, zl, y)]
    mate_s = [h * 2 + (1 - c), (1 - h) * 2 + c, (1 - h) * 2 + (1 - c)]
    mate_xl = [xl, 1 - xl, 1 - xl]
    mate_c = [1 - c, c, 1 - c]
    xc_dev = dev(3 - x, zh, c, zl, y)
    zl_dev = dev(x, zh, c, 1 - zl, y)
    y_dev = [dev(x, zh, c, zl, (y + d) % 4) for d in (1, 2, 3)]
    yz_dev = [dev(x, zh, c, 1 - zl, (y + d) % 4) for d in (1, 2, 3)]
    zh_dev = [dev(x, (zh + d) % 4, c, zl, y) for d in (1, 2, 3)]
    peer_dev = y_dev + [zl_dev] + yz_dev
    peer_ex = [zl * 4 + (y + d) % 4 for d in (1, 2, 3)] + [
        (1 - zl) * 4 + (y + d) % 4 for d in (0, 1, 2, 3)
    ]

    started, got, own = [], [], []

    class Copy:
        def __init__(self, key, src, dst, ssem, rsem, to):
            self.key = key
            self.d = pltpu.make_async_remote_copy(
                src_ref=src, dst_ref=dst, send_sem=ssem, recv_sem=rsem, device_id=to,
                device_id_type=MESH,
            )

        def start(self):
            assert self.key not in started
            started.append(self.key)
            self.d.start()

        def wait_recv(self):
            assert self.key not in got
            got.append(self.key)
            self.d.wait_recv()

        def wait_send(self):
            self.d.wait_send()

    def ck(k):
        return pl.ds(OFF[k], WIDTHS[k])

    def cols(start, size):
        return pl.ds(pl.multiple_of(start, 128), size)

    def info_mate(r):
        ref = INF.at[zl, s]
        return Copy((info_mate, r), ref, ref, is_s.at[r], is_r.at[r], mate_dev[r])

    def info_peer(i):
        ref = INE.at[ex]
        return Copy((info_peer, i), ref, ref, ie_s.at[i], ie_r.at[i], peer_dev[i])

    def info_z():
        ref = INF.at[zl]
        return Copy((info_z,), ref, ref, iz_s, iz_r, zl_dev)

    def q_copy(k, r):
        src = g_ref.at[:, cols(mate_s[r] * QW + OFF[k], WIDTHS[k])]
        return Copy((q_copy, k, r), src, T.at[zl, s, :, ck(k)], q_s.at[k, r], q_r.at[k, r], mate_dev[r])

    def z_copy(k):
        ref = T.at[zl, :, :, ck(k)]
        return Copy((z_copy, k), ref, ref, z_s.at[k], z_r.at[k], zl_dev)

    def y_copy(k, o, d):
        zz = zl if o == 0 else 1 - zl
        return Copy(
            (y_copy, k, o, d), SB.at[zz, (y + d) % 4, :, :, ck(k)], RB.at[:, zz, y, :, ck(k)],
            y_s.at[k, o, d - 1], y_r.at[k, o, d - 1], y_dev[d - 1],
        )

    def y_own(k, o):
        zz = zl if o == 0 else 1 - zl
        return pltpu.make_async_copy(
            SB.at[zz, y, :, :, ck(k)], RB.at[:, zz, y, :, ck(k)], y_l.at[k, o]
        )

    def x_copy(k):
        return Copy((x_copy, k), PX.at[:, ck(k)], XR.at[:, ck(k)], x_s.at[k], x_r.at[k], xc_dev)

    def zh_copy(k, d):
        return Copy(
            (zh_copy, k, d), ZS.at[(zh + d) % 4, :, :, ck(k)], ZR.at[d - 1, :, :, ck(k)],
            zh_s.at[k, d - 1], zh_r.at[k, d - 1], zh_dev[d - 1],
        )

    def f_copy(k, r):
        return Copy(
            (f_copy, k, r), FS.at[mate_xl[r], mate_c[r], :, ck(k)], FR.at[s, :, ck(k)],
            f_s.at[k, r], f_r.at[k, r], mate_dev[r],
        )

    def h_copy(i):
        ref = HQ.at[mate_s[1] if i == 2 else s]
        return Copy((h_copy, i), ref, ref, h_s.at[i], h_r.at[i], mate_dev[1 if i == 1 else 0])

    def w_copy(r):
        src = WB.at[:, cols(mate_s[r] * QW, QW)]
        return Copy((w_copy, r), src, WQ.at[x, zh, c], w_s.at[r], w_r.at[r], mate_dev[r])

    half = QW // 2
    pair = pl.ds(px * 2, 2)

    def wz_copy(i):
        ref = WQ.at[pair, zh]
        return Copy((wz_copy, i), ref, ref, wz_s.at[i], wz_r.at[i], zh_dev[0 if i == 0 else 2])

    def wf_copy(i):
        blk = (zh + 3) % 4 if i == 0 else (zh + 1) % 4
        ref = WQ.at[pair, blk, :, :, pl.ds(i * half, half)]
        return Copy((wf_copy, i), ref, ref, wf_s.at[i], wf_r.at[i], zh_dev[0 if i == 0 else 2])

    def wx_copy(d):
        ref = WQ.at[pair, (zh + d) % 4]
        return Copy((wx_copy, d), ref, ref, wx_s.at[d], wx_r.at[d], xc_dev)

    NB = 4
    BW = 1024 // NB

    def slab_cols(u):
        n = (px * 2 if u < 2 else 2 - px * 2) + u % 2
        return cols(n * BW, BW)

    def g1_copy(i, u):
        sl = slab_cols(u)
        return Copy(
            (g1_copy, i, u), GS1.at[i, :, sl], GR1.at[i, :, sl], g1_s.at[i, u], g1_r.at[i, u], mate_dev[0]
        )

    def g2_copy(u):
        sl = slab_cols(u)
        return Copy((g2_copy, u), GX.at[:, sl], GR2.at[:, sl], g2_s.at[u], g2_r.at[u], mate_dev[1])

    def b_copy(i):
        return Copy((b_copy, i), RG.at[peer_ex[i]], BK.at[ex], b_s.at[i], b_r.at[i], peer_dev[i])

    def loads():
        return [
            pltpu.make_async_copy(g_ref.at[:, cols(s * QW, QW)], T.at[zl, s], l_s.at[0]),
            pltpu.make_async_copy(mas_hbm, MAS, l_s.at[1]),
            pltpu.make_async_copy(hid_hbm, HID, l_s.at[2]),
        ]

    barrier = pltpu.get_barrier_semaphore()
    everyone = mate_dev + [xc_dev] + peer_dev + zh_dev
    for to in everyone:
        pl.semaphore_signal(barrier, inc=1, device_id=to, device_id_type=MESH)
    for cp in loads():
        cp.start()

    sub = lax.broadcasted_iota(jnp.int32, (8, 128), 0).astype(F32)
    ids0, ids1 = ids_ref[0:1, :].astype(F32), ids_ref[1:2, :].astype(F32)
    prob = prob_ref[...].astype(F32)
    oh0 = (sub == ids0).astype(F32)
    oh1 = (sub == ids1).astype(F32)
    tri = (
        lax.broadcasted_iota(jnp.int32, (128, 128), 0) < lax.broadcasted_iota(jnp.int32, (128, 128), 1)
    ).astype(BF16)
    before = jnp.dot((oh0 + oh1).astype(BF16), tri, preferred_element_type=F32)
    t0 = ids0 * float(CAP) + jnp.sum(oh0 * before, axis=0, keepdims=True)
    t1 = ids1 * float(CAP) + jnp.sum(oh1 * before, axis=0, keepdims=True)
    mine = jnp.where(
        sub == 0.0, t0, jnp.where(sub == 1.0, t1, jnp.where(sub == 2.0, prob[0:1, :], prob[1:2, :]))
    )
    INF[zl, s] = mine
    INE[ex] = mine

    pl.semaphore_wait(barrier, len(everyone))

    def stage_info():
        for r in (1, 2, 0):
            info_mate(r).start()

    def stage_peer():
        for i in range(7):
            info_peer(i).start()

    def stage_w0():
        loads()[1].wait()
        WB[...] = MAS[...].astype(BF16)
        for r in (1, 2, 0):
            w_copy(r).start()
        WQ[x, zh, c] = WB[:, cols(s * QW, QW)]

    def stage_q(k):
        for r in (1, 2, 0):
            q_copy(k, r).start()

    def onehot(zz):
        rows = lax.broadcasted_iota(jnp.int32, (4 * CAP, 128), 0) + zl * (4 * CAP)
        rows = rows.astype(F32)
        for ss in range(4):
            inf = INF[zz, ss]
            hit = (rows == inf[0:1, :]) | (rows == inf[1:2, :])
            SO[zz, ss] = jnp.where(hit, 1.0, 0.0).astype(BF16)

    def stage_o0():
        for r in range(3):
            info_mate(r).wait_recv()
        info_z().start()
        onehot(zl)

    def stage_o1():
        info_z().wait_recv()
        onehot(1 - zl)

    def stage_h():
        for i in range(7):
            info_peer(i).wait_recv()
        loads()[2].wait()
        rows = (lax.broadcasted_iota(jnp.int32, (CAP, 128), 0) + ex * CAP).astype(F32)
        for j in range(8):
            inf = INE[j]
            w = jnp.where(rows == inf[0:1, :], inf[2:3, :], 0.0) + jnp.where(
                rows == inf[1:2, :], inf[3:4, :], 0.0
            )
            p = jnp.sum(w, axis=1, keepdims=True)
            PC[j * CAP:(j + 1) * CAP, :] = jnp.broadcast_to(p, (CAP, 128))
            HQ[s, j * CAP:(j + 1) * CAP, :] = (
                HID[j * CAP:(j + 1) * CAP, :].astype(F32) * p
            ).astype(BF16)
        h_copy(1).start()
        h_copy(0).start()

    def stage_hf():
        h_copy(1).wait_recv()
        h_copy(2).start()

    def stage_ht():
        h_copy(0).wait_recv()
        h_copy(2).wait_recv()
        for ss in range(4):
            HT[:, ss * 384:(ss + 1) * 384] = HQ[ss].T

    def stage_b(k):
        for r in range(3):
            q_copy(k, r).wait_recv()
        if k == 0:
            loads()[0].wait()
        z_copy(k).start()

    def dispatch(k, o):
        zz = zl if o == 0 else 1 - zl
        for ss in range(4):
            out = jnp.dot(SO[zz, ss], T[zz, ss, :, ck(k)], preferred_element_type=F32).astype(BF16)
            for yy in range(4):
                SB[zz, yy, ss, :, ck(k)] = out[yy * CAP:(yy + 1) * CAP]
        for d in (2, 1, 3):
            y_copy(k, o, d).start()
        y_own(k, o).start()
        own.append((k, o))

    def stage_a(k):
        dispatch(k, 0)

    def stage_c(k):
        z_copy(k).wait_recv()
        dispatch(k, 1)

    def stage_d(k):
        for o in range(2):
            y_own(k, o).wait()
            own.remove((k, o))
            for d in (1, 2, 3):
                y_copy(k, o, d).wait_recv()
        rb = RB[:, :, :, :, ck(k)].reshape(4 * 384, WIDTHS[k])
        there = jnp.dot(HT[pl.ds((1 - px) * 512, 512), :], rb, preferred_element_type=F32)
        PX[:, ck(k)] = there.astype(BF16)
        x_copy(k).start()
        PO[:, ck(k)] = jnp.dot(HT[pl.ds(px * 512, 512), :], rb, preferred_element_type=F32)

    def stage_e(k):
        x_copy(k).wait_recv()
        tot = (PO[:, ck(k)] + XR[:, ck(k)].astype(F32)).astype(BF16).reshape(2, 4, 64, WIDTHS[k])
        for a in range(2):
            for b in range(4):
                ZS[b, a, :, ck(k)] = tot[a, b]
        for d in (2, 1, 3):
            zh_copy(k, d).start()

    def stage_f(k):
        for d in (1, 2, 3):
            zh_copy(k, d).wait_recv()
        tot = ZS[zh, :, :, ck(k)].astype(F32)
        for d in range(3):
            tot = tot + ZR[d, :, :, ck(k)].astype(F32)
        FS[:, :, :, ck(k)] = tot.astype(BF16).reshape(2, 2, 32, WIDTHS[k])
        for r in (1, 2, 0):
            f_copy(k, r).start()
        FR[s, :, ck(k)] = FS[xl, c, :, ck(k)]

    def stage_w1():
        for r in range(3):
            w_copy(r).wait_recv()
        wx_copy(0).start()
        for i in range(2):
            wz_copy(i).start()

    def stage_w2():
        for i in range(2):
            wz_copy(i).wait_recv()
            wf_copy(i).start()
        wx_copy(3).start()
        wx_copy(1).start()

    def stage_w3():
        for i in range(2):
            wf_copy(i).wait_recv()
        wx_copy(2).start()

    def stage_w4():
        for d in range(4):
            wx_copy(d).wait_recv()

    nt = (((1,), (1,)), ((), ()))

    def gdot(row, n):
        wn = WQ[n].reshape(BW, QW)
        return lax.dot_general(RB[row].reshape(384, QW), wn, nt, preferred_element_type=F32)

    def blk(i):
        return [i * 2, i * 2 + 1], [(px * 2 if i == 0 else 2 - px * 2) + a for a in range(2)]

    def stage_g1(i):
        for u, n in zip(*blk(i)):
            sl = cols(n * BW, BW)
            GS1[0, :, sl] = gdot(mate_s[2], n).astype(BF16)
            g1_copy(0, u).start()
            GO1[:, sl] = gdot(mate_s[1], n)

    def stage_g2(i):
        for u, n in zip(*blk(i)):
            sl = cols(n * BW, BW)
            g1_copy(0, u).wait_recv()
            GX[:, sl] = (GO1[:, sl] + GR1[0, :, sl].astype(F32)).astype(BF16)
            g2_copy(u).start()

    def stage_g3():
        for i in range(2):
            for u, n in zip(*blk(i)):
                sl = cols(n * BW, BW)
                GS1[1, :, sl] = gdot(mate_s[0], n).astype(BF16)
                g1_copy(1, u).start()
                GO[:, sl] = gdot(s, n)

    def stage_gr():
        for n in range(NB):
            g1_copy(1, n).wait_recv()
        for n in range(NB):
            g2_copy(n).wait_recv()
        for j in range(8):
            sl = slice(j * CAP, (j + 1) * CAP)
            tot = GO[sl, :] + GR1[1, sl, :].astype(F32) + GR2[sl, :].astype(F32)
            rg = jnp.sum(HID[sl, :].astype(F32) * tot, axis=1, keepdims=True)
            RG[j] = jnp.broadcast_to(rg, (CAP, 128))
            gh_ref[sl, :] = (tot * PC[sl, 0:1]).astype(BF16)
        for i in range(7):
            b_copy(i).start()
        BK[ex] = RG[ex]

    def stage_gp():
        for i in range(7):
            b_copy(i).wait_recv()
        inf = INE[ex]
        acc0 = jnp.zeros((1, 128), F32)
        acc1 = jnp.zeros((1, 128), F32)
        base = lax.broadcasted_iota(jnp.int32, (CAP, 128), 0).astype(F32)
        for e in range(8):
            rows = base + float(e * CAP)
            acc0 += jnp.sum(jnp.where(rows == inf[0:1, :], BK[e], 0.0), axis=0, keepdims=True)
            acc1 += jnp.sum(jnp.where(rows == inf[1:2, :], BK[e], 0.0), axis=0, keepdims=True)
        gp_ref[0:1, :] = acc0
        gp_ref[1:2, :] = acc1

    def stage_end():
        for k in range(NC):
            for r in range(3):
                f_copy(k, r).wait_recv()
        for q in range(4):
            gr_ref[:, q * QW:(q + 1) * QW] = FR[q]

    fns = dict(
        info=stage_info, peer=stage_peer, w0=stage_w0, q=stage_q, o0=stage_o0, o1=stage_o1, h=stage_h, hf=stage_hf, ht=stage_ht, a=stage_a, b=stage_b,
        c=stage_c, d=stage_d, e=stage_e, f=stage_f, w1=stage_w1, w2=stage_w2, w3=stage_w3,
        w4=stage_w4, g1=stage_g1, g2=stage_g2, g3=stage_g3, gr=stage_gr, gp=stage_gp, end=stage_end,
    )
    for name, *k in ORDER:
        fns[name](*k)

    for k in own:
        y_own(*k).wait()
    names = [item[0] for item in ORDER]
    for i, name in enumerate(("b", "w0", "h")):
        if name not in names:
            loads()[i].wait()
    for fn, *a in started:
        if (fn, *a) not in got:
            fn(*a).wait_recv()
        fn(*a).wait_send()


ORDER = [
    ("q", 0), ("info",), ("q", 1), ("w0",), ("q", 2), ("b", 0), ("b", 1), ("peer",), ("q", 3),
    ("o0",), ("w1",), ("q", 4), ("q", 5), ("a", 1), ("q", 6), ("b", 2), ("b", 3), ("a", 3),
    ("o1",), ("a", 2), ("b", 4), ("c", 1), ("h",), ("b", 5), ("b", 6), ("a", 5), ("a", 0),
    ("c", 0), ("a", 4), ("w2",), ("c", 2), ("hf",), ("c", 3), ("ht",), ("q", 7), ("a", 6),
    ("d", 1), ("d", 2), ("d", 3), ("c", 5), ("b", 7), ("d", 0), ("c", 6), ("a", 7), ("c", 4),
    ("e", 2), ("w3",), ("e", 3), ("d", 6), ("e", 0), ("c", 7), ("d", 5), ("d", 4), ("e", 1),
    ("d", 7), ("g1", 0), ("g2", 0), ("e", 6), ("w4",), ("g1", 1), ("e", 5), ("g2", 1), ("e", 4),
    ("f", 3), ("g3",), ("e", 7), ("f", 6), ("f", 5), ("f", 0), ("f", 1), ("f", 2), ("gr",),
    ("f", 4), ("f", 7), ("gp",), ("end",),
]


def per_device(grad_output, hidden, probs, expert_ids, master, first_moment, second_moment):
    width = grad_output.shape[1]
    qw = width // 4
    nc = len(WIDTHS)
    slab = hidden.shape[4]
    rows = hidden.shape[2] * hidden.shape[3]
    vm = pl.BlockSpec(memory_space=pltpu.VMEM)
    hbm = pl.BlockSpec(memory_space=pl.ANY)
    dma = pltpu.SemaphoreType.DMA
    scratch = [
        pltpu.VMEM((2, 4, 8, 128), F32),
        pltpu.VMEM((8, 8, 128), F32),
        pltpu.VMEM((2, 4, 128, qw), BF16),
        pltpu.VMEM((2, 4, 4 * CAP, 128), BF16),
        pltpu.VMEM((2, 4, 4, CAP, qw), BF16),
        pltpu.VMEM((4, 2, 4, CAP, qw), BF16),
        pltpu.VMEM((rows, 128), F32),
        pltpu.VMEM((rows, slab), BF16),
        pltpu.VMEM((32, width), F32),
        pltpu.VMEM((4, rows, slab), BF16),
        pltpu.VMEM((slab, 4 * rows), BF16),
        pltpu.VMEM((32, width), BF16),
        pltpu.VMEM((4, 4, 2, 32, qw), BF16),
        pltpu.VMEM((512, qw), BF16),
        pltpu.VMEM((512, qw), F32),
        pltpu.VMEM((512, qw), BF16),
        pltpu.VMEM((4, 2, 64, qw), BF16),
        pltpu.VMEM((3, 2, 64, qw), BF16),
        pltpu.VMEM((2, 2, 32, qw), BF16),
        pltpu.VMEM((4, 32, qw), BF16),
        pltpu.VMEM((2, rows, slab), BF16),
        pltpu.VMEM((2, rows, slab), BF16),
        pltpu.VMEM((rows, slab), F32),
        pltpu.VMEM((rows, slab), BF16),
        pltpu.VMEM((rows, slab), BF16),
        pltpu.VMEM((rows, slab), F32),
        pltpu.VMEM((8, CAP, 128), F32),
        pltpu.VMEM((8, CAP, 128), F32),
        dma((3,)),
        dma((3,)), dma((3,)), dma((7,)), dma((7,)), dma, dma,
        dma((nc, 3)), dma((nc, 3)), dma((nc,)), dma((nc,)),
        dma((nc, 2, 3)), dma((nc, 2, 3)), dma((nc, 2)),
        dma((nc,)), dma((nc,)), dma((nc, 3)), dma((nc, 3)), dma((nc, 3)), dma((nc, 3)),
        dma((3,)), dma((3,)), dma((3,)), dma((3,)),
        dma((2,)), dma((2,)), dma((2,)), dma((2,)), dma((4,)), dma((4,)),
        dma((2, 4)), dma((2, 4)), dma((4,)), dma((4,)), dma((7,)), dma((7,)),
    ]
    gh, gp, gr = pl.pallas_call(
        kernel,
        out_shape=(
            jax.ShapeDtypeStruct((rows, slab), BF16),
            jax.ShapeDtypeStruct((2, 128), F32),
            jax.ShapeDtypeStruct((32, width), BF16),
        ),
        in_specs=[vm, vm, hbm, hbm, hbm],
        out_specs=(vm, vm, vm),
        scratch_shapes=scratch,
        compiler_params=pltpu.CompilerParams(
            collective_id=0, has_side_effects=True, vmem_limit_bytes=60 * 1024 * 1024
        ),
        cost_estimate=pl.CostEstimate(
            flops=10 * 10**9, bytes_accessed=8 * 10**6, transcendentals=0
        ),
    )(expert_ids.T, probs.T, grad_output, hidden.reshape(rows, slab), master.reshape(32, width))
    grad_hidden = gh.reshape(hidden.shape)
    grad_probs = gp.T
    grad = gr.astype(F32).reshape(master.shape)
    new_first = 0.9 * first_moment + 0.1 * grad
    new_second = 0.95 * second_moment + 0.05 * grad * grad
    first_hat = new_first / (1.0 - 0.9**50)
    second_hat = new_second / (1.0 - 0.95**50)
    new_master = master - 0.0003 * (first_hat / (jnp.sqrt(second_hat) + 1e-08) + 0.1 * master)
    return (grad_hidden, grad_probs, new_master, new_first, new_second)


def solution(mesh):
    in_specs = (
        P(("dp", "expert"), None),
        P("dp", "expert", None, None, None),
        P(("dp", "expert"), None),
        P(("dp", "expert"), None),
        P("expert", "dp", None),
        P("expert", "dp", None),
        P("expert", "dp", None),
    )
    out_specs = (
        P("dp", "expert", None, None, None),
        P(("dp", "expert"), None),
        P("expert", "dp", None),
        P("expert", "dp", None),
        P("expert", "dp", None),
    )
    return jax.shard_map(
        per_device, mesh=mesh, in_specs=in_specs, out_specs=out_specs, check_vma=False
    )
```

time: 399 us -> 123 us (0.31)
  waiting for transfers between devices: 283 us -> 0 us
  Pallas kernels: 0 us -> 118 us
  matrix products: 28.8 us -> 0 us
  local copies, waits for them, and re-layouts: 29.8 us -> 1.46 us
  starting transfers between devices: 22.4 us -> 0 us
  other arithmetic: 19.5 us -> 2.85 us
  between operations: 14.2 us -> 0.7 us
    reduce_scatter x1 -> x0, waiting for transfers between devices: 142 us -> none  [per_device(): lax.psum_scatter(lax.dot_general(activations, scaled, (((0,), (0,)), ((),...]
    pallas_call x0 -> x1, Pallas kernels: none -> 118 us  [per_device(): pl.pallas_call(kernel, out_shape=(jax.ShapeDtypeStruct((rows, slab), BF16...]
    all_gather x1 -> x0, waiting for transfers between devices: 86.9 us -> none  [per_device(): gathered = lax.all_gather(weights_b, 'dp', axis=0, tiled=True)]
    all_to_all x3 -> x0, waiting for transfers between devices: 54.3 us -> none  [the longest x1 54.3 us: per_device(): lax.all_to_all(send_rows.reshape(experts_here, capacity, model_width), 'e...]
    dot_general x3 -> x0, matrix products: 28.8 us -> none  [the longest x1 10.3 us: per_device(): lax.dot_general(scaled, gathered, (((1,), (1,)), ((), ())), preferred_ele...]
    all_to_all x3 -> x0, starting transfers between devices: 22.1 us -> none  [the longest x1 10.6 us: per_device(): lax.all_to_all(row_grad, 'expert', split_axis=0, concat_axis=0, tiled=True)]
    unnamed x17 -> x12, local copies, waits for them, and re-layouts: 18.3 us -> 1.46 us
    convert_element_type x5 -> x0, other arithmetic: 9.88 us -> none  [the longest x2 9.85 us: per_device(): scaled = (got_probs.reshape(routed_rows, 1).astype(jnp.float32) * routed....]
  transfers between devices with their start and end apart: 5 -> 0, of which waited for: 3 -> 0; matrix products, arithmetic and copies ran while one was open for 7% -> 0% of each run, Pallas kernels for 0% -> 0%
where the time goes in v1:
time: 123 us
  Pallas kernels  118 us (96%)
  other arithmetic  2.85 us (2%)
  local copies, waits for them, and re-layouts  1.46 us (1%)
    pallas_call x1, Pallas kernels, per_device(): pl.pallas_call(kernel, out_shape=(jax.ShapeDtypeStruct((rows, slab), BF16...  118 us
    sub x1, other arithmetic, per_device(): master - 0.0003 * (first_hat / (jnp.sqrt(second_hat) + 1e-08) + 0.1 * mas...  2.85 us

profile of v1, /device:TPU:1, one launch (start us, length us, event | category | flops | bytes accessed | tf_op | source)
XLA Modules:
  0.0 123.3 jit_solution(8204412084633943733)
XLA Ops:
  0.6 0.0 copy-start
  0.6 0.0 copy-start.1
  0.7 0.0 copy-start.2
  0.7 118.3 %shard_map.110 = (bf16[384,1024]{1,0:T(8,128)(2,1)}, f32[2,128]{1,0:T(2,128)}, bf16[32,6144]{1,0:T(8,128)(2,1)}) custom-call(s32[2,128]{1,0:T(2,128)} %bitcast.20, bf16[2,128]{1,0:T(2,128)(2,1)} %bitcast.21, bf16[128,6144]{1,0:T(8,128)(2,1)} %g_ref.1, bf16[384,1024]{1,0:T(8,128)(2,1)} %bitcast.19, f32[32,6144]{1,0:T(8,128)} %bitcast.16), custom_call_target="tpu_custom_call" | custom-call | flops 10000000000 | bytes 8000000 | tf_op jit(solution)/shard_map/pallas_call | solution.py:498
  118.9 0.0 copy-done
  118.9 0.0 copy-done.1
  118.9 0.0 copy-done.2
  119.0 0.0 copy-start.3
  119.0 2.8 %multiply_subtract_fusion = (f32[1,32,6144]{2,1,0:T(8,128)}, f32[1,32,6144]{2,1,0:T(8,128)}, f32[1,32,6144]{2,1,0:T(8,128)}) fusion(f32[1,32,6144]{2,1,0:T(8,128)S(1)} %copy-done, bf16[32,6144]{1,0:T(8,128)(2,1)} %get-tuple-element.10, f32[1,32,6144]{2,1,0:T(8,128)S(1)} %copy-done.1, f32[1,32,6144]{2,1,0:T(8,128)S(1)} %copy-done.2), kind=kLoop, calls=%fused_computation.6 | loop fusion | flops 3145728 | bytes 5111808 | tf_op jit(solution)/shard_map/sub | solution.py:522
  121.8 0.0 copy-start.4
  121.8 0.0 copy-done.3
  121.8 0.9 copy.14
  122.7 0.0 copy-done.4
  122.7 0.6 copy.15
Async XLA Ops:
  0.6 118.3 %copy-start = (f32[1,32,6144]{2,1,0:T(8,128)S(1)}, f32[1,32,6144]{2,1,0:T(8,128)}, u32[]{:S(2)}) copy-start(f32[1,32,6144]{2,1,0:T(8,128)} %param.11) | copy-start | bytes 2359300
  0.6 118.3 %copy-start.1 = (f32[1,32,6144]{2,1,0:T(8,128)S(1)}, f32[1,32,6144]{2,1,0:T(8,128)}, u32[]{:S(2)}) copy-start(f32[1,32,6144]{2,1,0:T(8,128)} %param.12) | copy-start | bytes 2359300
  0.7 118.3 %copy-start.2 = (f32[1,32,6144]{2,1,0:T(8,128)S(1)}, f32[1,32,6144]{2,1,0:T(8,128)}, u32[]{:S(2)}) copy-start(f32[1,32,6144]{2,1,0:T(8,128)} %param.13) | copy-start | bytes 2359300
  119.0 2.9 %copy-start.3 = (bf16[384,1024]{1,0:T(8,128)(2,1)S(1)}, bf16[384,1024]{1,0:T(8,128)(2,1)}, u32[]{:S(2)}) copy-start(bf16[384,1024]{1,0:T(8,128)(2,1)} %get-tuple-element.8) | copy-start | bytes 2359300
  121.8 0.9 copy-start.4

commit v2 on v1

--- a/solution.py
+++ b/solution.py
@@ -9,16 +9,17 @@
 F32 = jnp.float32
 BF16 = jnp.bfloat16
 CAP = 48
+RING = [0, 1, 2, 3, 4, 5]
 WIDTHS = [128, 128, 256, 256, 256, 256, 128, 128]
 
 
 def kernel(
     ids_ref, prob_ref, g_ref, hid_hbm, mas_hbm,
     gh_ref, gp_ref, gr_ref,
-    INF, INE, T, SO, SB, RB, PC, HID, MAS, HQ, HT, WB, WQ, PX, PO, XR, ZS, ZR, FS, FR,
+    INF, INE, T, SO, SB, RB, PC, HID, MAS, HQ, HT, WB, WQ, PX, PO, XR, ZS, ZR, ZH, FS, FR,
     GS1, GR1, GO1, GX, GR2, GO, RG, BK,
-    l_s, is_s, is_r, ie_s, ie_r, iz_s, iz_r, q_s, q_r, z_s, z_r, y_s, y_r, y_l, x_s, x_r, zh_s, zh_r,
-    f_s, f_r, h_s, h_r, w_s, w_r, wz_s, wz_r, wf_s, wf_r, wx_s, wx_r, g1_s, g1_r, g2_s, g2_r, b_s, b_r,
+    l_s, is_s, is_r, ie_s, ie_r, iz_s, iz_r, q_s, q_r, z_s, z_r, y_s, y_r, y_l, x_s, x_r, zh_s, zh_r, zn_s, zn_r, za_s, za_r,
+    f_s, f_r, h_s, h_r, w_s, w_r, wz_s, wz_r, wf_s, wf_r, wx_s, wx_r, wp_s, wp_r, g1_s, g1_r, g2_s, g2_r, b_s, b_r,
 ):
     QW = RB.shape[4]
     NC = len(WIDTHS)
@@ -49,7 +50,7 @@
         (1 - zl) * 4 + (y + d) % 4 for d in (0, 1, 2, 3)
     ]
 
-    started, got, own = [], [], []
+    started, got, sent, own = [], [], [], []
 
     class Copy:
         def __init__(self, key, src, dst, ssem, rsem, to):
@@ -70,6 +71,8 @@
             self.d.wait_recv()
 
         def wait_send(self):
+            assert self.key in started and self.key not in sent
+            sent.append(self.key)
             self.d.wait_send()
 
     def ck(k):
@@ -120,15 +123,38 @@
             zh_s.at[k, d - 1], zh_r.at[k, d - 1], zh_dev[d - 1],
         )
 
+    ring_dev = [zh_dev[0], zh_dev[2]]
+
+    def zr_copy(k, i):
+        return Copy(
+            (zr_copy, k, i), ZS.at[(zh + 2) % 4, i, :, ck(k)], ZH.at[i, :, ck(k)],
+            zh_s.at[k, i], zh_r.at[k, i], ring_dev[i],
+        )
+
+    def zn_copy(k, i):
+        return Copy(
+            (zn_copy, k, i), ZS.at[(zh + 1 + 2 * i) % 4, 1 - i, :, ck(k)], ZR.at[i, 1 - i, :, ck(k)],
+            zn_s.at[k, i], zn_r.at[k, i], ring_dev[i],
+        )
+
+    def za_copy(k, i):
+        return Copy(
+            (za_copy, k, i), ZS.at[(zh + 1 + 2 * i) % 4, i, :, ck(k)], ZR.at[i, i, :, ck(k)],
+            za_s.at[k, i], za_r.at[k, i], ring_dev[i],
+        )
+
     def f_copy(k, r):
         return Copy(
             (f_copy, k, r), FS.at[mate_xl[r], mate_c[r], :, ck(k)], FR.at[s, :, ck(k)],
             f_s.at[k, r], f_r.at[k, r], mate_dev[r],
         )
 
-    def h_copy(i):
-        ref = HQ.at[mate_s[1] if i == 2 else s]
-        return Copy((h_copy, i), ref, ref, h_s.at[i], h_r.at[i], mate_dev[1 if i == 1 else 0])
+    def h_copy(i, p=0):
+        if i == 0:
+            ref = HQ.at[s]
+        else:
+            ref = HQ.at[s if i == 1 else mate_s[1], pl.ds(p * 96, 96)]
+        return Copy((h_copy, i, p), ref, ref, h_s.at[i, p], h_r.at[i, p], mate_dev[1 if i == 1 else 0])
 
     def w_copy(r):
         src = WB.at[:, cols(mate_s[r] * QW, QW)]
@@ -137,18 +163,27 @@
     half = QW // 2
     pair = pl.ds(px * 2, 2)
 
-    def wz_copy(i):
-        ref = WQ.at[pair, zh]
-        return Copy((wz_copy, i), ref, ref, wz_s.at[i], wz_r.at[i], zh_dev[0 if i == 0 else 2])
+    def ring_blk(i):
+        return (zh + 3 + 2 * i) % 4
+
+    def half_cols(i):
+        return pl.ds(i * half, half)
+
+    def wz_copy(p, i):
+        ref = WQ.at[pair, zh, :, :, half_cols((i + p) % 2)]
+        return Copy((wz_copy, p, i), ref, ref, wz_s.at[p, i], wz_r.at[p, i], ring_dev[i])
 
     def wf_copy(i):
-        blk = (zh + 3) % 4 if i == 0 else (zh + 1) % 4
-        ref = WQ.at[pair, blk, :, :, pl.ds(i * half, half)]
-        return Copy((wf_copy, i), ref, ref, wf_s.at[i], wf_r.at[i], zh_dev[0 if i == 0 else 2])
+        ref = WQ.at[pair, ring_blk(i), :, :, half_cols(i)]
+        return Copy((wf_copy, i), ref, ref, wf_s.at[i], wf_r.at[i], ring_dev[i])
 
     def wx_copy(d):
         ref = WQ.at[pair, (zh + d) % 4]
         return Copy((wx_copy, d), ref, ref, wx_s.at[d], wx_r.at[d], xc_dev)
+
+    def wp_copy(p, i):
+        ref = WQ.at[pair, ring_blk(i), :, :, half_cols((i + p) % 2)]
+        return Copy((wp_copy, p, i), ref, ref, wp_s.at[p, i], wp_r.at[p, i], xc_dev)
 
     NB = 4
     BW = 1024 // NB
@@ -255,16 +290,20 @@
             HQ[s, j * CAP:(j + 1) * CAP, :] = (
                 HID[j * CAP:(j + 1) * CAP, :].astype(F32) * p
             ).astype(BF16)
-        h_copy(1).start()
         h_copy(0).start()
 
+    def stage_hp(p):
+        h_copy(1, p).start()
+
     def stage_hf():
-        h_copy(1).wait_recv()
-        h_copy(2).start()
+        for p in range(4):
+            h_copy(1, p).wait_recv()
+            h_copy(2, p).start()
 
     def stage_ht():
         h_copy(0).wait_recv()
-        h_copy(2).wait_recv()
+        for p in range(4):
+            h_copy(2, p).wait_recv()
         for ss in range(4):
             HT[:, ss * 384:(ss + 1) * 384] = HQ[ss].T
 
@@ -311,33 +350,70 @@
         for a in range(2):
             for b in range(4):
                 ZS[b, a, :, ck(k)] = tot[a, b]
-        for d in (2, 1, 3):
-            zh_copy(k, d).start()
+        if k in RING:
+            for i in range(2):
+                zr_copy(k, i).start()
+            for i in range(2):
+                zn_copy(k, i).start()
+        else:
+            for d in (2, 1, 3):
+                zh_copy(k, d).start()
+
+    def stage_e2(k):
+        for i in range(2):
+            zr_copy(k, i).wait_recv()
+            blk = (zh + 1 + 2 * i) % 4
+            tot = ZS[blk, i, :, ck(k)].astype(F32) + ZH[i, :, ck(k)].astype(F32)
+            ZS[blk, i, :, ck(k)] = tot.astype(BF16)
+            za_copy(k, i).start()
 
     def stage_f(k):
-        for d in (1, 2, 3):
-            zh_copy(k, d).wait_recv()
+        if k in RING:
+            for i in range(2):
+                zn_copy(k, i).wait_recv()
+                za_copy(k, i).wait_recv()
+        else:
+            for d in (1, 2, 3):
+                zh_copy(k, d).wait_recv()
         tot = ZS[zh, :, :, ck(k)].astype(F32)
-        for d in range(3):
+        for d in range(2 if k in RING else 3):
             tot = tot + ZR[d, :, :, ck(k)].astype(F32)
         FS[:, :, :, ck(k)] = tot.astype(BF16).reshape(2, 2, 32, WIDTHS[k])
         for r in (1, 2, 0):
             f_copy(k, r).start()
         FR[s, :, ck(k)] = FS[xl, c, :, ck(k)]
 
+    def quad_weights():
+        for r in range(3):
+            if (w_copy, r) not in got:
+                w_copy(r).wait_recv()
+
     def stage_w1():
-        for r in range(3):
-            w_copy(r).wait_recv()
+        quad_weights()
         wx_copy(0).start()
-        for i in range(2):
-            wz_copy(i).start()
+
+    def stage_wa():
+        quad_weights()
+        for i in range(2):
+            wz_copy(0, i).start()
+
+    def stage_wb():
+        for i in range(2):
+            wz_copy(1, i).start()
 
     def stage_w2():
         for i in range(2):
-            wz_copy(i).wait_recv()
+            wz_copy(0, i).wait_recv()
             wf_copy(i).start()
-        wx_copy(3).start()
-        wx_copy(1).start()
+
+    def stage_w2x():
+        for i in range(2):
+            wp_copy(0, i).start()
+
+    def stage_w2y():
+        for i in range(2):
+            wz_copy(1, i).wait_recv()
+            wp_copy(1, i).start()
 
     def stage_w3():
         for i in range(2):
@@ -345,8 +421,45 @@
         wx_copy(2).start()
 
     def stage_w4():
-        for d in range(4):
+        for d in (0, 2):
             wx_copy(d).wait_recv()
+        for p in range(2):
+            for i in range(2):
+                wp_copy(p, i).wait_recv()
+
+    def stage_dr(k):
+        for r in range(3):
+            q_copy(k, r).wait_send()
+        z_copy(k).wait_send()
+        for o in range(2):
+            for d in (1, 2, 3):
+                y_copy(k, o, d).wait_send()
+
+    def stage_ds(k):
+        x_copy(k).wait_send()
+        if k in RING:
+            for i in range(2):
+                zr_copy(k, i).wait_send()
+                zn_copy(k, i).wait_send()
+        else:
+            for d in (1, 2, 3):
+                zh_copy(k, d).wait_send()
+
+    def stage_dw():
+        info_z().wait_send()
+        for r in range(3):
+            info_mate(r).wait_send()
+            w_copy(r).wait_send()
+        h_copy(0).wait_send()
+        for p in range(4):
+            h_copy(1, p).wait_send()
+            h_copy(2, p).wait_send()
+        for i in range(7):
+            info_peer(i).wait_send()
+        for i in range(2):
+            wz_copy(0, i).wait_send()
+            wz_copy(1, i).wait_send()
+            wf_copy(i).wait_send()
 
     nt = (((1,), (1,)), ((), ()))
 
@@ -416,8 +529,9 @@
             gr_ref[:, q * QW:(q + 1) * QW] = FR[q]
 
     fns = dict(
-        info=stage_info, peer=stage_peer, w0=stage_w0, q=stage_q, o0=stage_o0, o1=stage_o1, h=stage_h, hf=stage_hf, ht=stage_ht, a=stage_a, b=stage_b,
-        c=stage_c, d=stage_d, e=stage_e, f=stage_f, w1=stage_w1, w2=stage_w2, w3=stage_w3,
+        info=stage_info, peer=stage_peer, w0=stage_w0, q=stage_q, o0=stage_o0, o1=stage_o1, h=stage_h, hp=stage_hp, hf=stage_hf, ht=stage_ht, a=stage_a, b=stage_b,
+        c=stage_c, d=stage_d, e=stage_e, f=stage_f, w1=stage_w1, w2=stage_w2, w3=stage_w3, wa=stage_wa, wb=stage_wb, w2x=stage_w2x, w2y=stage_w2y,
+        e2=stage_e2, dr=stage_dr, ds=stage_ds, dw=stage_dw,
         w4=stage_w4, g1=stage_g1, g2=stage_g2, g3=stage_g3, gr=stage_gr, gp=stage_gp, end=stage_end,
     )
     for name, *k in ORDER:
@@ -432,19 +546,22 @@
     for fn, *a in started:
         if (fn, *a) not in got:
             fn(*a).wait_recv()
-        fn(*a).wait_send()
+        if (fn, *a) not in sent:
+            fn(*a).wait_send()
 
 
 ORDER = [
-    ("q", 0), ("info",), ("q", 1), ("w0",), ("q", 2), ("b", 0), ("b", 1), ("peer",), ("q", 3),
-    ("o0",), ("w1",), ("q", 4), ("q", 5), ("a", 1), ("q", 6), ("b", 2), ("b", 3), ("a", 3),
-    ("o1",), ("a", 2), ("b", 4), ("c", 1), ("h",), ("b", 5), ("b", 6), ("a", 5), ("a", 0),
-    ("c", 0), ("a", 4), ("w2",), ("c", 2), ("hf",), ("c", 3), ("ht",), ("q", 7), ("a", 6),
-    ("d", 1), ("d", 2), ("d", 3), ("c", 5), ("b", 7), ("d", 0), ("c", 6), ("a", 7), ("c", 4),
-    ("e", 2), ("w3",), ("e", 3), ("d", 6), ("e", 0), ("c", 7), ("d", 5), ("d", 4), ("e", 1),
-    ("d", 7), ("g1", 0), ("g2", 0), ("e", 6), ("w4",), ("g1", 1), ("e", 5), ("g2", 1), ("e", 4),
-    ("f", 3), ("g3",), ("e", 7), ("f", 6), ("f", 5), ("f", 0), ("f", 1), ("f", 2), ("gr",),
-    ("f", 4), ("f", 7), ("gp",), ("end",),
+    ("q", 0), ("info",), ("q", 1), ("w0",), ("q", 2), ("q", 3), ("q", 4), ("q", 5), ("b", 0),
+    ("peer",), ("q", 6), ("o0",), ("b", 1), ("a", 0), ("wa",), ("w1",), ("a", 1), ("o1",),
+    ("wb",), ("h",), ("hp", 0), ("hp", 1), ("c", 0), ("b", 2), ("c", 1), ("b", 3), ("b", 4),
+    ("a", 2), ("b", 5), ("a", 4), ("hp", 2), ("b", 6), ("hp", 3), ("w2",), ("w2x",), ("a", 3),
+    ("w2y",), ("q", 7), ("c", 2), ("hf",), ("a", 6), ("ht",), ("d", 1), ("c", 3), ("d", 0),
+    ("a", 5), ("b", 7), ("d", 2), ("c", 5), ("e", 1), ("d", 3), ("e", 0), ("c", 6), ("c", 4),
+    ("e", 2), ("d", 5), ("a", 7), ("w3",), ("d", 6), ("c", 7), ("e2", 1), ("e", 3), ("d", 4),
+    ("e", 5), ("d", 7), ("g1", 0), ("f", 1), ("e2", 0), ("e2", 2), ("g2", 0), ("e2", 3),
+    ("w4",), ("g1", 1), ("e", 6), ("e2", 5), ("g2", 1), ("f", 0), ("f", 2), ("g3",), ("e", 4),
+    ("f", 6), ("f", 3), ("f", 5), ("e", 7), ("e2", 4), ("gr",), ("f", 7), ("f", 4), ("gp",),
+    ("end",),
 ]
 
 
@@ -476,6 +593,7 @@
         pltpu.VMEM((512, qw), BF16),
         pltpu.VMEM((4, 2, 64, qw), BF16),
         pltpu.VMEM((3, 2, 64, qw), BF16),
+        pltpu.VMEM((2, 64, qw), BF16),
         pltpu.VMEM((2, 2, 32, qw), BF16),
         pltpu.VMEM((4, 32, qw), BF16),
         pltpu.VMEM((2, rows, slab), BF16),
@@ -490,9 +608,11 @@
         dma((3,)), dma((3,)), dma((7,)), dma((7,)), dma, dma,
         dma((nc, 3)), dma((nc, 3)), dma((nc,)), dma((nc,)),
         dma((nc, 2, 3)), dma((nc, 2, 3)), dma((nc, 2)),
-        dma((nc,)), dma((nc,)), dma((nc, 3)), dma((nc, 3)), dma((nc, 3)), dma((nc, 3)),
-        dma((3,)), dma((3,)), dma((3,)), dma((3,)),
-        dma((2,)), dma((2,)), dma((2,)), dma((2,)), dma((4,)), dma((4,)),
+        dma((nc,)), dma((nc,)), dma((nc, 3)), dma((nc, 3)),
+        dma((nc, 2)), dma((nc, 2)), dma((nc, 2)), dma((nc, 2)), dma((nc, 3)), dma((nc, 3)),
+        dma((3, 4)), dma((3, 4)), dma((3,)), dma((3,)),
+        dma((2, 2)), dma((2, 2)), dma((2,)), dma((2,)), dma((4,)), dma((4,)),
+        dma((2, 2)), dma((2, 2)),
         dma((2, 4)), dma((2, 4)), dma((4,)), dma((4,)), dma((7,)), dma((7,)),
     ]
     gh, gp, gr = pl.pallas_call(

time: 123 us -> 123 us (level)
  no operation moved by 1% of the time
where the time goes in v2:
time: 123 us
  Pallas kernels  118 us (96%)
  other arithmetic  2.85 us (2%)
  local copies, waits for them, and re-layouts  1.46 us (1%)
    pallas_call x1, Pallas kernels, per_device(): pl.pallas_call(kernel, out_shape=(jax.ShapeDtypeStruct((rows, slab), BF16...  118 us
    sub x1, other arithmetic, per_device(): master - 0.0003 * (first_hat / (jnp.sqrt(second_hat) + 1e-08) + 0.1 * mas...  2.85 us

profile of v2, /device:TPU:1, one launch (start us, length us, event | category | flops | bytes accessed | tf_op | source)
XLA Modules:
  0.0 122.9 jit_solution(16013477300431548485)
XLA Ops:
  0.6 0.0 copy-start
  0.6 0.0 copy-start.1
  0.7 0.0 copy-start.2
  0.7 117.9 %shard_map.110 = (bf16[384,1024]{1,0:T(8,128)(2,1)}, f32[2,128]{1,0:T(2,128)}, bf16[32,6144]{1,0:T(8,128)(2,1)}) custom-call(s32[2,128]{1,0:T(2,128)} %bitcast.20, bf16[2,128]{1,0:T(2,128)(2,1)} %bitcast.21, bf16[128,6144]{1,0:T(8,128)(2,1)} %g_ref.1, bf16[384,1024]{1,0:T(8,128)(2,1)} %bitcast.19, f32[32,6144]{1,0:T(8,128)} %bitcast.16), custom_call_target="tpu_custom_call" | custom-call | flops 10000000000 | bytes 8000000 | tf_op jit(solution)/shard_map/pallas_call | solution.py:618
  118.6 0.0 copy-done
  118.6 0.0 copy-done.1
  118.6 0.0 copy-done.2
  118.6 0.0 copy-start.3
  118.6 2.8 %multiply_subtract_fusion = (f32[1,32,6144]{2,1,0:T(8,128)}, f32[1,32,6144]{2,1,0:T(8,128)}, f32[1,32,6144]{2,1,0:T(8,128)}) fusion(f32[1,32,6144]{2,1,0:T(8,128)S(1)} %copy-done, bf16[32,6144]{1,0:T(8,128)(2,1)} %get-tuple-element.10, f32[1,32,6144]{2,1,0:T(8,128)S(1)} %copy-done.1, f32[1,32,6144]{2,1,0:T(8,128)S(1)} %copy-done.2), kind=kLoop, calls=%fused_computation.6 | loop fusion | flops 3145728 | bytes 5111808 | tf_op jit(solution)/shard_map/sub | solution.py:642
  121.4 0.0 copy-start.4
  121.5 0.0 copy-done.3
  121.5 0.9 copy.14
  122.3 0.0 copy-done.4
  122.3 0.6 copy.15
Async XLA Ops:
  0.6 117.9 %copy-start = (f32[1,32,6144]{2,1,0:T(8,128)S(1)}, f32[1,32,6144]{2,1,0:T(8,128)}, u32[]{:S(2)}) copy-start(f32[1,32,6144]{2,1,0:T(8,128)} %param.11) | copy-start | bytes 2359300
  0.6 117.9 %copy-start.1 = (f32[1,32,6144]{2,1,0:T(8,128)S(1)}, f32[1,32,6144]{2,1,0:T(8,128)}, u32[]{:S(2)}) copy-start(f32[1,32,6144]{2,1,0:T(8,128)} %param.12) | copy-start | bytes 2359300
  0.7 117.9 %copy-start.2 = (f32[1,32,6144]{2,1,0:T(8,128)S(1)}, f32[1,32,6144]{2,1,0:T(8,128)}, u32[]{:S(2)}) copy-start(f32[1,32,6144]{2,1,0:T(8,128)} %param.13) | copy-start | bytes 2359300
  118.6 2.9 %copy-start.3 = (bf16[384,1024]{1,0:T(8,128)(2,1)S(1)}, bf16[384,1024]{1,0:T(8,128)(2,1)}, u32[]{:S(2)}) copy-start(bf16[384,1024]{1,0:T(8,128)(2,1)} %get-tuple-element.8) | copy-start | bytes 2359300
  121.4 0.9 copy-start.4
